TPU v7x, 32 devices: a whole 2x2x4 slice. The times are simulated.
32 devices in a mesh: dev: 32 (over z, y, x, core).
Axes of the slice: x: 2, y: 2, z: 4, core: 2. Of those that a mesh axis runs over, the one named last changes fastest.
Arguments:
- right_sides: float32 [32, 64, 512], P('dev'), may hold values from -6 to 6
- diag_inverse: float32 [64, 512, 512], P('dev'), may hold values from -0.25 to 0.25
- factor_tiles: float32 [256, 512, 512], P('dev'), may hold values from -0.09375 to 0.09375
- node_level: int32 [64], replicated, may hold values from 0 to 4, as said below
- tile_column: int32 [256], replicated, may hold values from 0 to 63, as said below
- tile_row: int32 [256], replicated, may hold values from 0 to 63, as said below
Outputs:
- solution: float32 [32, 64, 512], P('dev')
Inputs may be any that keep to these rules, and one draw needn't show every extreme that they name: `node_level`: supernode s is owned by device s // 2; the 2 supernodes of one device lie at different levels, and every level holds supernodes of two or more devices. `tile_column`: tile k is held by device k // 8; its column supernode lies at a lower level than its row supernode. Among one device's tiles whose column supernodes lie at one level there are at most 4 tiles, 2 distinct column supernodes and 2 distinct row supernodes; some device reaches all three bounds. A pair of supernodes may recur on several tiles. `tile_row`: drawn together with tile_column, under its bounds.
All inputs are finite; a program needn't handle non-finite values.
Results may differ from a plain program's by a relative error of at most 0.0001.
Values sent between devices are 32-bit elements; how exact they have to be, the bound alone decides.
A program may use at most 128 MiB of HBM per device.

v0:
```python
import jax
import jax.numpy as jnp
from jax import lax
from jax.sharding import PartitionSpec as P

LEVELS = 5
TCAP = 4


full_precision = lax.Precision.HIGHEST


def lookup(table, indices):
    positions = jnp.arange(table.shape[0], dtype=jnp.int32)
    return jnp.sum(jnp.where(indices[..., None] == positions, table, 0), axis=-1)


def slot_table(labels, active, capacity):
    entries = labels.shape[1]
    place_ids = jnp.arange(entries, dtype=jnp.int32)
    alike = labels[:, :, None] == labels[:, None, :]
    earlier = alike & active[:, None, :] & (place_ids[None, None, :] < place_ids[None, :, None])
    leading = active & jnp.logical_not(jnp.any(earlier, axis=2))
    rank_of = jnp.cumsum(leading.astype(jnp.int32), axis=1) - 1
    matches = alike & leading[:, None, :]
    tile_slot = jnp.sum(jnp.where(matches, rank_of[:, None, :], 0), axis=2)
    slot_ids = jnp.arange(capacity, dtype=jnp.int32)
    chosen_hit = leading[:, :, None] & (rank_of[:, :, None] == slot_ids)
    slot_key = jnp.sum(jnp.where(chosen_hit, labels[:, :, None], 0), axis=1)
    slot_valid = jnp.any(chosen_hit, axis=1)
    return (tile_slot, slot_key, slot_valid)


def gather_rows(field, indices, validity):
    picked = jnp.take(field, indices, axis=1)
    return jnp.where(validity[None, :, None], picked, 0.0)


def scatter_rows(field, indices, validity, payload):
    placed = jnp.where(validity, indices, field.shape[1])
    return field.at[:, placed, :].add(payload, mode="drop")


def per_device(right_sides, diag_inverse, factor_tiles, node_level, tile_column, tile_row):
    devices = lax.axis_size("dev")
    myself = lax.axis_index("dev")
    columns = right_sides.shape[0]
    per_owner = diag_inverse.shape[0]
    per_holder = factor_tiles.shape[0]
    block_size = factor_tiles.shape[1]
    tile_level = lookup(node_level, tile_column)
    owner_levels = node_level.reshape(devices, per_owner)
    holder_levels = tile_level.reshape(devices, per_holder)
    holder_index = jnp.broadcast_to(jnp.arange(per_holder, dtype=jnp.int32), (devices, per_holder))
    holder_base = jnp.arange(devices, dtype=jnp.int32)[:, None] * per_holder
    solution = jnp.zeros_like(right_sides)
    update = jnp.zeros_like(right_sides)
    for current in range(LEVELS):
        at_level = owner_levels == current
        has_one = jnp.any(at_level, axis=1)
        local_slot = jnp.sum(jnp.where(at_level, jnp.arange(per_owner, dtype=jnp.int32), 0), axis=1)
        targets = jnp.arange(devices, dtype=jnp.int32) * per_owner + local_slot
        residue = gather_rows(right_sides, targets, has_one) - gather_rows(update, targets, has_one)
        outgoing = residue[:, :, None, :]
        my_slot = lax.dynamic_index_in_dim(local_slot, myself, 0, keepdims=False)
        inverse = lax.dynamic_index_in_dim(diag_inverse, my_slot, 0, keepdims=False)

        def solve_items(pieces, inverse=inverse):
            return jnp.einsum("rnkb,bc->rnkc", pieces, inverse, precision=full_precision)

        solved = solve_items(
            lax.all_to_all(outgoing, "dev", split_axis=1, concat_axis=1, tiled=True)
        )
        returned = lax.all_to_all(solved, "dev", split_axis=1, concat_axis=1, tiled=True)
        solution = scatter_rows(solution, targets, has_one, returned[:, :, 0, :])
        if current + 1 < LEVELS:
            active = holder_levels == current
            tile_rank, slot_tile, slot_valid = slot_table(holder_index, active, TCAP)
            global_tile = holder_base + slot_tile
            slot_column = lookup(tile_column, global_tile)
            slot_row = lookup(tile_row, global_tile)
            carried = gather_rows(
                solution, slot_column.reshape(-1), slot_valid.reshape(-1)
            ).reshape(columns, devices, TCAP, block_size)
            tile_ids = slot_tile[None, :, :]
            payload = lax.all_to_all(carried, "dev", split_axis=1, concat_axis=1, tiled=True)
            names = lax.all_to_all(tile_ids, "dev", split_axis=1, concat_axis=1, tiled=True)
            chosen = jnp.take(factor_tiles, names[0, 0], axis=0)
            products = jnp.einsum("rnkb,kbc->rnkc", payload, chosen, precision=full_precision)
            coming = lax.all_to_all(products, "dev", split_axis=1, concat_axis=1, tiled=True)
            update = scatter_rows(
                update,
                slot_row.reshape(-1),
                slot_valid.reshape(-1),
                coming.reshape(columns, devices * TCAP, block_size),
            )
    return solution


def solution(mesh):
    placed = (P("dev", None, None), P("dev", None, None), P("dev", None, None), P(), P(), P())
    return jax.shard_map(
        per_device, mesh=mesh, in_specs=placed, out_specs=P("dev", None, None), check_vma=False
    )
```

profile of v0, /device:TPU:0, one launch (start us, length us, event | category | flops | bytes accessed | tf_op | source)
XLA Modules:
  0.0 300.7 jit_solution(6042720270658952077)
XLA Ops:
  4.2 7.3 %all-to-all-start = ((f32[1,32,1,512]{3,2,0,1:T(1,128)}), f32[1,32,1,512]{3,2,0,1:T(1,128)S(1)}, u32[]{:S(2)}, u32[]{:S(2)}) async-start(f32[1,32,1,512]{3,2,0,1:T(1,128)} %copy.53), calls=%async_computation | async-start | bytes 131072 | tf_op jit(solution)/shard_map/all_to_all | solution.py:72
  20.3 5.7 %all-to-all-start.1 = ((f32[1,32,1,512]{3,2,0,1:T(1,128)}), f32[1,32,1,512]{3,2,0,1:T(1,128)S(1)}, u32[]{:S(2)}, u32[]{:S(2)}) async-start(f32[1,32,1,512]{3,2,0,1:T(1,128)} %copy.54), calls=%async_computation.1 | async-start | bytes 131072 | tf_op jit(solution)/shard_map/all_to_all | solution.py:74
  28.8 4.6 %all-to-all-done.1 = f32[1,32,1,512]{3,2,0,1:T(1,128)S(1)} async-done(((f32[1,32,1,512]{3,2,0,1:T(1,128)}), f32[1,32,1,512]{3,2,0,1:T(1,128)S(1)}, u32[]{:S(2)}, u32[]{:S(2)}) %all-to-all-start.1) | async-done | bytes 65568 | tf_op jit(solution)/shard_map/all_to_all | solution.py:74
  38.5 4.7 %all-to-all-done.2 = s32[1,32,4]{2,0,1:T(1,128)S(1)} async-done(((s32[1,32,4]{2,0,1:T(1,128)}), s32[1,32,4]{2,0,1:T(1,128)S(1)}, u32[]{:S(2)}, u32[]{:S(2)}) %all-to-all-start.2) | async-done | bytes 544 | tf_op jit(solution)/shard_map/all_to_all | solution.py:87
  43.2 2.6 all-to-all-start.3
  45.8 6.1 %gather_fusion.3 = f32[4,512,512]{2,1,0:T(8,128)} fusion(f32[8,512,512]{2,1,0:T(8,128)} %param.14, s32[1024]{0:T(1024)S(1)} %pad_clamp_fusion.10), kind=kCustom, calls=%fused_computation.1.clone | custom fusion | bytes 8388624 | tf_op jit(solution)/shard_map/jit(_take)/gather | solution.py:88
  51.9 4.4 %all-to-all-done.3 = f32[1,32,4,512]{3,2,0,1:T(4,128)S(1)} async-done(((f32[1,32,4,512]{3,2,0,1:T(4,128)}), f32[1,32,4,512]{3,2,0,1:T(4,128)S(1)}, u32[]{:S(2)}, u32[]{:S(2)}) %all-to-all-start.3) | async-done | bytes 262176 | tf_op jit(solution)/shard_map/all_to_all | solution.py:86
  56.3 5.1 %fusion.16 = f32[1,32,4,512]{3,1,2,0:T(8,128)S(1)} fusion(f32[4,512,512]{2,1,0:T(8,128)} %gather_fusion.3, pred[4]{0:T(512)(128)(4,1)S(1)} %get-tuple-element.46, f32[1,32,4,512]{3,2,0,1:T(4,128)S(1)} %all-to-all-done.3), kind=kOutput, calls=%fused_computation.43 | convolution fusion | flops 403701760 | bytes 4718596 | tf_op jit(solution)/shard_map/rnkb,kbc->rnkc/dot_general | solution.py:89
  62.3 2.6 all-to-all-start.4
  64.9 10.5 %all-to-all-done.4 = f32[1,32,4,512]{3,2,0,1:T(4,128)S(1)} async-done(((f32[1,32,4,512]{3,2,0,1:T(4,128)}), f32[1,32,4,512]{3,2,0,1:T(4,128)S(1)}, u32[]{:S(2)}, u32[]{:S(2)}) %all-to-all-start.4) | async-done | bytes 262176 | tf_op jit(solution)/shard_map/all_to_all | solution.py:90
  78.3 2.6 all-to-all-start.5
  83.7 4.6 %all-to-all-done.5 = f32[1,32,1,512]{3,2,0,1:T(1,128)S(1)} async-done(((f32[1,32,1,512]{3,2,0,1:T(1,128)}), f32[1,32,1,512]{3,2,0,1:T(1,128)S(1)}, u32[]{:S(2)}, u32[]{:S(2)}) %all-to-all-start.5) | async-done | bytes 65568 | tf_op jit(solution)/shard_map/all_to_all | solution.py:72
  89.7 2.6 all-to-all-start.6
  96.7 3.0 all-to-all-done.6
  99.7 2.9 all-to-all-start.7
  105.1 4.6 %all-to-all-done.7 = s32[1,32,4]{2,0,1:T(1,128)S(1)} async-done(((s32[1,32,4]{2,0,1:T(1,128)}), s32[1,32,4]{2,0,1:T(1,128)S(1)}, u32[]{:S(2)}, u32[]{:S(2)}) %all-to-all-start.7) | async-done | bytes 544 | tf_op jit(solution)/shard_map/all_to_all | solution.py:87
  109.7 2.8 all-to-all-start.8
  112.6 6.1 %gather_fusion.7 = f32[4,512,512]{2,1,0:T(8,128)} fusion(f32[8,512,512]{2,1,0:T(8,128)} %param.14, s32[1024]{0:T(1024)S(1)} %pad_clamp_fusion.7), kind=kCustom, calls=%fused_computation.12.clone | custom fusion | bytes 8388624 | tf_op jit(solution)/shard_map/jit(_take)/gather | solution.py:88
  118.7 4.3 %all-to-all-done.8 = f32[1,32,4,512]{3,2,0,1:T(4,128)S(1)} async-done(((f32[1,32,4,512]{3,2,0,1:T(4,128)}), f32[1,32,4,512]{3,2,0,1:T(4,128)S(1)}, u32[]{:S(2)}, u32[]{:S(2)}) %all-to-all-start.8) | async-done | bytes 262176 | tf_op jit(solution)/shard_map/all_to_all | solution.py:86
  122.9 5.0 %fusion.19 = f32[1,32,4,512]{3,1,2,0:T(8,128)S(1)} fusion(f32[4,512,512]{2,1,0:T(8,128)} %gather_fusion.7, pred[4]{0:T(512)(128)(4,1)S(1)} %get-tuple-element.42, f32[1,32,4,512]{3,2,0,1:T(4,128)S(1)} %all-to-all-done.8), kind=kOutput, calls=%fused_computation.44 | convolution fusion | flops 403701760 | bytes 4718596 | tf_op jit(solution)/shard_map/rnkb,kbc->rnkc/dot_general | solution.py:89
  128.8 2.6 all-to-all-start.9
  131.5 10.5 %all-to-all-done.9 = f32[1,32,4,512]{3,2,0,1:T(4,128)S(1)} async-done(((f32[1,32,4,512]{3,2,0,1:T(4,128)}), f32[1,32,4,512]{3,2,0,1:T(4,128)S(1)}, u32[]{:S(2)}, u32[]{:S(2)}) %all-to-all-start.9) | async-done | bytes 262176 | tf_op jit(solution)/shard_map/all_to_all | solution.py:90
  144.9 2.6 all-to-all-start.10
  147.5 7.4 %all-to-all-done.10 = f32[1,32,1,512]{3,2,0,1:T(1,128)S(1)} async-done(((f32[1,32,1,512]{3,2,0,1:T(1,128)}), f32[1,32,1,512]{3,2,0,1:T(1,128)S(1)}, u32[]{:S(2)}, u32[]{:S(2)}) %all-to-all-start.10) | async-done | bytes 65568 | tf_op jit(solution)/shard_map/all_to_all | solution.py:72
  156.3 2.6 all-to-all-start.11
  161.9 4.4 %all-to-all-done.11 = f32[1,32,1,512]{3,2,0,1:T(1,128)S(1)} async-done(((f32[1,32,1,512]{3,2,0,1:T(1,128)}), f32[1,32,1,512]{3,2,0,1:T(1,128)S(1)}, u32[]{:S(2)}, u32[]{:S(2)}) %all-to-all-start.11) | async-done | bytes 65568 | tf_op jit(solution)/shard_map/all_to_all | solution.py:74
  171.4 4.6 %all-to-all-done.12 = s32[1,32,4]{2,0,1:T(1,128)S(1)} async-done(((s32[1,32,4]{2,0,1:T(1,128)}), s32[1,32,4]{2,0,1:T(1,128)S(1)}, u32[]{:S(2)}, u32[]{:S(2)}) %all-to-all-start.12) | async-done | bytes 544 | tf_op jit(solution)/shard_map/all_to_all | solution.py:87
  176.0 2.6 all-to-all-start.13
  178.7 6.1 %gather_fusion.11 = f32[4,512,512]{2,1,0:T(8,128)} fusion(f32[8,512,512]{2,1,0:T(8,128)} %param.14, s32[1024]{0:T(1024)S(1)} %pad_clamp_fusion.4), kind=kCustom, calls=%fused_computation.13.clone | custom fusion | bytes 8388624 | tf_op jit(solution)/shard_map/jit(_take)/gather | solution.py:88
  184.8 4.4 %all-to-all-done.13 = f32[1,32,4,512]{3,2,0,1:T(4,128)S(1)} async-done(((f32[1,32,4,512]{3,2,0,1:T(4,128)}), f32[1,32,4,512]{3,2,0,1:T(4,128)S(1)}, u32[]{:S(2)}, u32[]{:S(2)}) %all-to-all-start.13) | async-done | bytes 262176 | tf_op jit(solution)/shard_map/all_to_all | solution.py:86
  189.2 5.0 %fusion.22 = f32[1,32,4,512]{3,1,2,0:T(8,128)S(1)} fusion(f32[4,512,512]{2,1,0:T(8,128)} %gather_fusion.11, pred[4]{0:T(512)(128)(4,1)S(1)} %get-tuple-element.38, f32[1,32,4,512]{3,2,0,1:T(4,128)S(1)} %all-to-all-done.13), kind=kOutput, calls=%fused_computation.45 | convolution fusion | flops 403701760 | bytes 4718596 | tf_op jit(solution)/shard_map/rnkb,kbc->rnkc/dot_general | solution.py:89
  195.1 2.6 all-to-all-start.14
  199.2 9.2 %all-to-all-done.14 = f32[1,32,4,512]{3,2,0,1:T(4,128)S(1)} async-done(((f32[1,32,4,512]{3,2,0,1:T(4,128)}), f32[1,32,4,512]{3,2,0,1:T(4,128)S(1)}, u32[]{:S(2)}, u32[]{:S(2)}) %all-to-all-start.14) | async-done | bytes 262176 | tf_op jit(solution)/shard_map/all_to_all | solution.py:90
  211.3 2.6 all-to-all-start.15
  213.8 7.4 %all-to-all-done.15 = f32[1,32,1,512]{3,2,0,1:T(1,128)S(1)} async-done(((f32[1,32,1,512]{3,2,0,1:T(1,128)}), f32[1,32,1,512]{3,2,0,1:T(1,128)S(1)}, u32[]{:S(2)}, u32[]{:S(2)}) %all-to-all-start.15) | async-done | bytes 65568 | tf_op jit(solution)/shard_map/all_to_all | solution.py:72
  222.6 2.6 all-to-all-start.16
  226.2 6.5 %all-to-all-done.16 = f32[1,32,1,512]{3,2,0,1:T(1,128)S(1)} async-done(((f32[1,32,1,512]{3,2,0,1:T(1,128)}), f32[1,32,1,512]{3,2,0,1:T(1,128)S(1)}, u32[]{:S(2)}, u32[]{:S(2)}) %all-to-all-start.16) | async-done | bytes 65568 | tf_op jit(solution)/shard_map/all_to_all | solution.py:74
  232.6 2.8 all-to-all-start.17
  237.9 4.6 %all-to-all-done.17 = s32[1,32,4]{2,0,1:T(1,128)S(1)} async-done(((s32[1,32,4]{2,0,1:T(1,128)}), s32[1,32,4]{2,0,1:T(1,128)S(1)}, u32[]{:S(2)}, u32[]{:S(2)}) %all-to-all-start.17) | async-done | bytes 544 | tf_op jit(solution)/shard_map/all_to_all | solution.py:87
  242.6 2.6 all-to-all-start.18
  245.8 6.1 %gather_fusion.15 = f32[4,512,512]{2,1,0:T(8,128)} fusion(f32[8,512,512]{2,1,0:T(8,128)} %param.14, s32[1024]{0:T(1024)S(1)} %pad_clamp_fusion.1), kind=kCustom, calls=%fused_computation.14.clone | custom fusion | bytes 8388624 | tf_op jit(solution)/shard_map/jit(_take)/gather | solution.py:88
  251.9 3.9 %all-to-all-done.18 = f32[1,32,4,512]{3,2,0,1:T(4,128)S(1)} async-done(((f32[1,32,4,512]{3,2,0,1:T(4,128)}), f32[1,32,4,512]{3,2,0,1:T(4,128)S(1)}, u32[]{:S(2)}, u32[]{:S(2)}) %all-to-all-start.18) | async-done | bytes 262176 | tf_op jit(solution)/shard_map/all_to_all | solution.py:86
  255.8 5.0 %fusion.25 = f32[1,32,4,512]{3,1,2,0:T(8,128)S(1)} fusion(f32[4,512,512]{2,1,0:T(8,128)} %gather_fusion.15, pred[4]{0:T(512)(128)(4,1)S(1)} %get-tuple-element.34, f32[1,32,4,512]{3,2,0,1:T(4,128)S(1)} %all-to-all-done.18), kind=kOutput, calls=%fused_computation.46 | convolution fusion | flops 403701760 | bytes 4718596 | tf_op jit(solution)/shard_map/rnkb,kbc->rnkc/dot_general | solution.py:89
  261.7 2.6 all-to-all-start.19
  264.9 10.0 %all-to-all-done.19 = f32[1,32,4,512]{3,2,0,1:T(4,128)S(1)} async-done(((f32[1,32,4,512]{3,2,0,1:T(4,128)}), f32[1,32,4,512]{3,2,0,1:T(4,128)S(1)}, u32[]{:S(2)}, u32[]{:S(2)}) %all-to-all-start.19) | async-done | bytes 262176 | tf_op jit(solution)/shard_map/all_to_all | solution.py:90
  277.8 2.6 all-to-all-start.20
  283.1 4.7 %all-to-all-done.20 = f32[1,32,1,512]{3,2,0,1:T(1,128)S(1)} async-done(((f32[1,32,1,512]{3,2,0,1:T(1,128)}), f32[1,32,1,512]{3,2,0,1:T(1,128)S(1)}, u32[]{:S(2)}, u32[]{:S(2)}) %all-to-all-start.20) | async-done | bytes 65568 | tf_op jit(solution)/shard_map/all_to_all | solution.py:72
  291.8 7.4 %all-to-all-done.21 = f32[1,32,1,512]{3,2,0,1:T(1,128)S(1)} async-done(((f32[1,32,1,512]{3,2,0,1:T(1,128)}), f32[1,32,1,512]{3,2,0,1:T(1,128)S(1)}, u32[]{:S(2)}, u32[]{:S(2)}) %all-to-all-start.21) | async-done | bytes 65568 | tf_op jit(solution)/shard_map/all_to_all | solution.py:74
  (195 shorter events, 62.1 us)
Async XLA Ops:
  0.0 18.9 %copy-start = (f32[2,512,512]{2,1,0:T(8,128)S(1)}, f32[2,512,512]{2,1,0:T(8,128)}, u32[]{:S(2)}) copy-start(f32[2,512,512]{2,1,0:T(8,128)} %param.13) | copy-start | bytes 6291460
  4.2 14.7 %all-to-all-start = ((f32[1,32,1,512]{3,2,0,1:T(1,128)}), f32[1,32,1,512]{3,2,0,1:T(1,128)S(1)}, u32[]{:S(2)}, u32[]{:S(2)}) async-start(f32[1,32,1,512]{3,2,0,1:T(1,128)} %copy.53), calls=%async_computation | async-start | bytes 131072 | tf_op jit(solution)/shard_map/all_to_all | solution.py:72
  20.3 13.2 %all-to-all-start.1 = ((f32[1,32,1,512]{3,2,0,1:T(1,128)}), f32[1,32,1,512]{3,2,0,1:T(1,128)S(1)}, u32[]{:S(2)}, u32[]{:S(2)}) async-start(f32[1,32,1,512]{3,2,0,1:T(1,128)} %copy.54), calls=%async_computation.1 | async-start | bytes 131072 | tf_op jit(solution)/shard_map/all_to_all | solution.py:74
  33.4 9.7 %all-to-all-start.2 = ((s32[1,32,4]{2,0,1:T(1,128)}), s32[1,32,4]{2,0,1:T(1,128)S(1)}, u32[]{:S(2)}, u32[]{:S(2)}) async-start(s32[1,32,4]{2,0,1:T(1,128)} %copy.58), calls=%async_computation.2 | async-start | bytes 32768 | tf_op jit(solution)/shard_map/all_to_all | solution.py:87
  43.2 13.2 %all-to-all-start.3 = ((f32[1,32,4,512]{3,2,0,1:T(4,128)}), f32[1,32,4,512]{3,2,0,1:T(4,128)S(1)}, u32[]{:S(2)}, u32[]{:S(2)}) async-start(f32[1,32,4,512]{3,2,0,1:T(4,128)} %reshape.1020), calls=%async_computation.3 | async-start | bytes 524288 | tf_op jit(solution)/shard_map/all_to_all | solution.py:86
  56.3 38.8 %copy-start.2 = (f32[1,64,512]{2,1,0:T(8,128)S(1)}, f32[1,64,512]{2,1,0:T(8,128)}, u32[]{:S(2)}) copy-start(f32[1,64,512]{2,1,0:T(8,128)} %param.12) | copy-start | bytes 393220
  62.3 13.2 %all-to-all-start.4 = ((f32[1,32,4,512]{3,2,0,1:T(4,128)}), f32[1,32,4,512]{3,2,0,1:T(4,128)S(1)}, u32[]{:S(2)}, u32[]{:S(2)}) async-start(f32[1,32,4,512]{3,2,0,1:T(4,128)} %copy.63), calls=%async_computation.4 | async-start | bytes 524288 | tf_op jit(solution)/shard_map/all_to_all | solution.py:90
  78.3 10.0 %all-to-all-start.5 = ((f32[1,32,1,512]{3,2,0,1:T(1,128)}), f32[1,32,1,512]{3,2,0,1:T(1,128)S(1)}, u32[]{:S(2)}, u32[]{:S(2)}) async-start(f32[1,32,1,512]{3,2,0,1:T(1,128)} %copy.64), calls=%async_computation.5 | async-start | bytes 131072 | tf_op jit(solution)/shard_map/all_to_all | solution.py:72
  89.7 10.0 %all-to-all-start.6 = ((f32[1,32,1,512]{3,2,0,1:T(1,128)}), f32[1,32,1,512]{3,2,0,1:T(1,128)S(1)}, u32[]{:S(2)}, u32[]{:S(2)}) async-start(f32[1,32,1,512]{3,2,0,1:T(1,128)} %copy.65), calls=%async_computation.6 | async-start | bytes 131072 | tf_op jit(solution)/shard_map/all_to_all | solution.py:74
  99.7 10.0 %all-to-all-start.7 = ((s32[1,32,4]{2,0,1:T(1,128)}), s32[1,32,4]{2,0,1:T(1,128)S(1)}, u32[]{:S(2)}, u32[]{:S(2)}) async-start(s32[1,32,4]{2,0,1:T(1,128)} %copy.69), calls=%async_computation.7 | async-start | bytes 32768 | tf_op jit(solution)/shard_map/all_to_all | solution.py:87
  109.7 13.2 %all-to-all-start.8 = ((f32[1,32,4,512]{3,2,0,1:T(4,128)}), f32[1,32,4,512]{3,2,0,1:T(4,128)S(1)}, u32[]{:S(2)}, u32[]{:S(2)}) async-start(f32[1,32,4,512]{3,2,0,1:T(4,128)} %reshape.1021), calls=%async_computation.8 | async-start | bytes 524288 | tf_op jit(solution)/shard_map/all_to_all | solution.py:86
  128.8 13.2 %all-to-all-start.9 = ((f32[1,32,4,512]{3,2,0,1:T(4,128)}), f32[1,32,4,512]{3,2,0,1:T(4,128)S(1)}, u32[]{:S(2)}, u32[]{:S(2)}) async-start(f32[1,32,4,512]{3,2,0,1:T(4,128)} %copy.74), calls=%async_computation.9 | async-start | bytes 524288 | tf_op jit(solution)/shard_map/all_to_all | solution.py:90
  144.9 10.0 %all-to-all-start.10 = ((f32[1,32,1,512]{3,2,0,1:T(1,128)}), f32[1,32,1,512]{3,2,0,1:T(1,128)S(1)}, u32[]{:S(2)}, u32[]{:S(2)}) async-start(f32[1,32,1,512]{3,2,0,1:T(1,128)} %copy.75), calls=%async_computation.10 | async-start | bytes 131072 | tf_op jit(solution)/shard_map/all_to_all | solution.py:72
  156.3 10.0 %all-to-all-start.11 = ((f32[1,32,1,512]{3,2,0,1:T(1,128)}), f32[1,32,1,512]{3,2,0,1:T(1,128)S(1)}, u32[]{:S(2)}, u32[]{:S(2)}) async-start(f32[1,32,1,512]{3,2,0,1:T(1,128)} %copy.76), calls=%async_computation.11 | async-start | bytes 131072 | tf_op jit(solution)/shard_map/all_to_all | solution.py:74
  166.3 9.7 %all-to-all-start.12 = ((s32[1,32,4]{2,0,1:T(1,128)}), s32[1,32,4]{2,0,1:T(1,128)S(1)}, u32[]{:S(2)}, u32[]{:S(2)}) async-start(s32[1,32,4]{2,0,1:T(1,128)} %copy.80), calls=%async_computation.12 | async-start | bytes 32768 | tf_op jit(solution)/shard_map/all_to_all | solution.py:87
  176.0 13.2 %all-to-all-start.13 = ((f32[1,32,4,512]{3,2,0,1:T(4,128)}), f32[1,32,4,512]{3,2,0,1:T(4,128)S(1)}, u32[]{:S(2)}, u32[]{:S(2)}) async-start(f32[1,32,4,512]{3,2,0,1:T(4,128)} %reshape.1022), calls=%async_computation.13 | async-start | bytes 524288 | tf_op jit(solution)/shard_map/all_to_all | solution.py:86
  195.1 13.2 %all-to-all-start.14 = ((f32[1,32,4,512]{3,2,0,1:T(4,128)}), f32[1,32,4,512]{3,2,0,1:T(4,128)S(1)}, u32[]{:S(2)}, u32[]{:S(2)}) async-start(f32[1,32,4,512]{3,2,0,1:T(4,128)} %copy.85), calls=%async_computation.14 | async-start | bytes 524288 | tf_op jit(solution)/shard_map/all_to_all | solution.py:90
  211.3 10.0 %all-to-all-start.15 = ((f32[1,32,1,512]{3,2,0,1:T(1,128)}), f32[1,32,1,512]{3,2,0,1:T(1,128)S(1)}, u32[]{:S(2)}, u32[]{:S(2)}) async-start(f32[1,32,1,512]{3,2,0,1:T(1,128)} %copy.86), calls=%async_computation.15 | async-start | bytes 131072 | tf_op jit(solution)/shard_map/all_to_all | solution.py:72
  222.6 10.0 %all-to-all-start.16 = ((f32[1,32,1,512]{3,2,0,1:T(1,128)}), f32[1,32,1,512]{3,2,0,1:T(1,128)S(1)}, u32[]{:S(2)}, u32[]{:S(2)}) async-start(f32[1,32,1,512]{3,2,0,1:T(1,128)} %copy.87), calls=%async_computation.16 | async-start | bytes 131072 | tf_op jit(solution)/shard_map/all_to_all | solution.py:74
  232.6 9.9 %all-to-all-start.17 = ((s32[1,32,4]{2,0,1:T(1,128)}), s32[1,32,4]{2,0,1:T(1,128)S(1)}, u32[]{:S(2)}, u32[]{:S(2)}) async-start(s32[1,32,4]{2,0,1:T(1,128)} %copy.91), calls=%async_computation.17 | async-start | bytes 32768 | tf_op jit(solution)/shard_map/all_to_all | solution.py:87
  242.6 13.2 %all-to-all-start.18 = ((f32[1,32,4,512]{3,2,0,1:T(4,128)}), f32[1,32,4,512]{3,2,0,1:T(4,128)S(1)}, u32[]{:S(2)}, u32[]{:S(2)}) async-start(f32[1,32,4,512]{3,2,0,1:T(4,128)} %reshape.1023), calls=%async_computation.18 | async-start | bytes 524288 | tf_op jit(solution)/shard_map/all_to_all | solution.py:86
  261.7 13.2 %all-to-all-start.19 = ((f32[1,32,4,512]{3,2,0,1:T(4,128)}), f32[1,32,4,512]{3,2,0,1:T(4,128)S(1)}, u32[]{:S(2)}, u32[]{:S(2)}) async-start(f32[1,32,4,512]{3,2,0,1:T(4,128)} %copy.96), calls=%async_computation.19 | async-start | bytes 524288 | tf_op jit(solution)/shard_map/all_to_all | solution.py:90
  277.8 10.0 %all-to-all-start.20 = ((f32[1,32,1,512]{3,2,0,1:T(1,128)}), f32[1,32,1,512]{3,2,0,1:T(1,128)S(1)}, u32[]{:S(2)}, u32[]{:S(2)}) async-start(f32[1,32,1,512]{3,2,0,1:T(1,128)} %copy.97), calls=%async_computation.20 | async-start | bytes 131072 | tf_op jit(solution)/shard_map/all_to_all | solution.py:72
  289.2 10.0 %all-to-all-start.21 = ((f32[1,32,1,512]{3,2,0,1:T(1,128)}), f32[1,32,1,512]{3,2,0,1:T(1,128)S(1)}, u32[]{:S(2)}, u32[]{:S(2)}) async-start(f32[1,32,1,512]{3,2,0,1:T(1,128)} %copy.98), calls=%async_computation.21 | async-start | bytes 131072 | tf_op jit(solution)/shard_map/all_to_all | solution.py:74
  300.0 0.7 copy-start.1
where the time goes:
time: 302 us; the launch traced here: 301 us
  waiting for transfers between devices  126 us (42%)
  starting transfers between devices  65.2 us (22%)
  local copies, waits for them, and re-layouts  59.5 us (20%)
  matrix products  23.7 us (8%)
  other arithmetic  15.7 us (5%)
  between operations  10.6 us (4%)
    all_to_all x4, waiting for transfers between devices, per_device(): lax.all_to_all(products, 'dev', split_axis=1, concat_axis=1, tiled=True)  40.2 us
    all_to_all x5, waiting for transfers between devices, per_device(): lax.all_to_all(solved, 'dev', split_axis=1, concat_axis=1, tiled=True)  25.9 us
    gather x4, local copies, waits for them, and re-layouts, per_device(): chosen = jnp.take(factor_tiles, names[0, 0], axis=0)  24.5 us
    all_to_all x5, waiting for transfers between devices, per_device(): lax.all_to_all(outgoing, 'dev', split_axis=1, concat_axis=1, tiled=True)  24.2 us
    dot_general x4, matrix products, per_device(): jnp.einsum('rnkb,kbc->rnkc', payload, chosen, precision=full_precision)  20.2 us
    all_to_all x4, waiting for transfers between devices, per_device(): lax.all_to_all(tile_ids, 'dev', split_axis=1, concat_axis=1, tiled=True)  18.6 us
    all_to_all x5, starting transfers between devices, per_device(): lax.all_to_all(outgoing, 'dev', split_axis=1, concat_axis=1, tiled=True)  17.6 us
    all_to_all x4, waiting for transfers between devices, per_device(): lax.all_to_all(carried, 'dev', split_axis=1, concat_axis=1, tiled=True)  17 us
  transfers between devices with their start and end apart: 22, of which 22 were waited for; matrix products, arithmetic and copies ran while one was open for 17% of the time, Pallas kernels for 0%

commit v1 on v0

v1 whole, which is shorter than its diff:
```python
import functools

import jax
import jax.numpy as jnp
from jax import lax
from jax.experimental import pallas as pl
from jax.experimental.pallas import tpu as pltpu
from jax.sharding import PartitionSpec as P

LEVELS = 5
TCAP = 4
MESH = pl.DeviceIdType.MESH
F32, BF16 = jnp.float32, jnp.bfloat16


def stack3(x):
    hi = x.astype(BF16)
    rest = x - hi.astype(F32)
    mid = rest.astype(BF16)
    lo = (rest - mid.astype(F32)).astype(BF16)
    return jnp.concatenate([hi, mid, lo], axis=0)


def dot(a, b):
    return jnp.dot(a, b, preferred_element_type=F32)


def kernel(n, tab, pick, drop, take, place, b_ref, dinv, tiles, out,
           stage, wh, wl, csplit, xsplit,
           s_res, r_res, s_sol, r_sol, s_car, r_car, s_pro, r_pro,
           load_sem, send_sem, recv_sem):
    me = lax.axis_index("dev")
    per_owner, per_holder = dinv.shape[0], tiles.shape[0]
    size = dinv.shape[1]

    loads = [pltpu.make_async_copy(dinv, stage.at[pl.ds(0, per_owner)], load_sem.at[0]),
             pltpu.make_async_copy(tiles, stage.at[pl.ds(per_owner, per_holder)], load_sem.at[1])]
    for c in loads:
        c.start()

    barrier = pltpu.get_barrier_semaphore()

    def greet(i, _):
        pl.semaphore_signal(barrier, inc=1, device_id=(lax.rem(me + i, n),), device_id_type=MESH)
        return 0

    lax.fori_loop(1, n, greet, 0)

    def begin(src, dst, k):
        def send(i, _):
            peer = lax.rem(me + i, n)
            pltpu.make_async_remote_copy(
                src_ref=src.at[peer], dst_ref=dst.at[me],
                send_sem=send_sem.at[k], recv_sem=recv_sem.at[k],
                device_id=(peer,), device_id_type=MESH).start()
            return 0

        lax.fori_loop(1, n, send, 0)
        dst[me] = src[me]

    def whole(src, dst, k):
        return pltpu.make_async_remote_copy(
            src_ref=src.at[pl.ds(0, n - 1)], dst_ref=dst.at[pl.ds(0, n - 1)],
            send_sem=send_sem.at[k], recv_sem=recv_sem.at[k],
            device_id=(lax.rem(me + 1, n),), device_id_type=MESH)

    def split(first, count):
        rows = 64
        per = size // rows

        def body(i, _):
            m, c = i // per, pl.multiple_of((i % per) * rows, rows)
            w = stage[first + m, pl.ds(c, rows), :]
            hi = w.astype(BF16)
            wh[first + m, pl.ds(c, rows), :] = hi
            wl[first + m, pl.ds(c, rows), :] = (w - hi.astype(F32)).astype(BF16)
            return 0

        lax.fori_loop(0, count * per, body, 0)

    def halves(x):
        hi = x.astype(BF16)
        return hi, (x - hi.astype(F32)).astype(BF16)

    def multiply(hi, lo, which):
        m = hi.shape[0]
        a = dot(jnp.concatenate([hi, lo], axis=0), wh[which])
        return a[:m] + a[m:] + dot(hi, wl[which])

    waits = []
    k = 0
    bsplit = stack3(b_ref[...])
    for level in range(LEVELS):
        res = dot(pick[level], bsplit)
        if level:
            width = 6 * n * level
            res = res - dot(drop[level, :, :width], csplit[:width])
        s_res[level] = res.reshape(n, 1, size)
        if level == 0:
            pl.semaphore_wait(barrier, n - 1)
        begin(s_res.at[level], r_res.at[level], k)
        if level == 0:
            loads[0].wait()
            split(0, per_owner)
        w = whole(s_res.at[level], r_res.at[level], k)
        w.wait_recv()
        waits.append(w)
        k += 1

        hi, lo = halves(r_res[level].reshape(n, size))
        s_sol[level] = multiply(hi, lo, tab[level]).reshape(n, 1, size)
        begin(s_sol.at[level], r_sol.at[level], k)
        if level == 0:
            loads[1].wait()
            split(per_owner, per_holder)
        w = whole(s_sol.at[level], r_sol.at[level], k)
        w.wait_recv()
        waits.append(w)
        k += 1

        xs = stack3(r_sol[level].reshape(n, size))
        xsplit[pl.ds(3 * n * level, 3 * n), :] = xs
        if level + 1 == LEVELS:
            break
        for j in range(2):
            s_car[level, :, j, :] = dot(take[level, j], xs)
        begin(s_car.at[level], r_car.at[level], k)
        w = whole(s_car.at[level], r_car.at[level], k)
        w.wait_recv()
        waits.append(w)
        k += 1

        sums = [jnp.zeros((n, size), F32), jnp.zeros((n, size), F32)]
        got = [r_car[level, :, j, :] for j in range(2)]
        for t in range(TCAP):
            at = LEVELS + (level * TCAP + t) * 4
            second = tab[at + 1].astype(F32)
            x = got[0] * (1.0 - second) + got[1] * second
            hi, lo = halves(x)
            y = multiply(hi, lo, tab[at])
            for j in range(2):
                sums[j] += y * tab[at + 2 + j].astype(F32)
        for j in range(2):
            s_pro[level, :, j, :] = sums[j]
        begin(s_pro.at[level], r_pro.at[level], k)
        w = whole(s_pro.at[level], r_pro.at[level], k)
        w.wait_recv()
        waits.append(w)
        k += 1
        for j in range(2):
            csplit[pl.ds(3 * n * (2 * level + j), 3 * n), :] = stack3(r_pro[level, :, j, :])

    out[...] = dot(place[...], xsplit[...])
    for w in waits:
        w.wait_send()


def plan(n, node_level, tile_column, tile_row, per_owner, per_holder):
    ns = node_level.shape[0]
    level_of = jnp.sum(jnp.where(tile_column[:, None] == jnp.arange(ns, dtype=jnp.int32), node_level, 0), axis=1)
    lev = level_of.reshape(n, per_holder)
    col, row = tile_column.reshape(n, per_holder), tile_row.reshape(n, per_holder)
    steps = jnp.arange(LEVELS - 1, dtype=jnp.int32)
    act = lev[None] == steps[:, None, None]
    ends = lambda v: jnp.stack([jnp.min(jnp.where(act, v, 1 << 20), axis=2),
                                jnp.max(jnp.where(act, v, -1), axis=2)], axis=1)
    cset, rset = ends(col), ends(row)
    dev = jnp.arange(n, dtype=jnp.int32)
    nodes = jnp.arange(ns, dtype=jnp.int32)
    every = jnp.arange(LEVELS, dtype=jnp.int32)
    owned = node_level.reshape(n, per_owner)
    hit = owned[None] == every[:, None, None]
    ids = nodes.reshape(n, per_owner)
    target = jnp.max(jnp.where(hit, ids, -7), axis=2)
    own_slot = jnp.max(jnp.where(hit, jnp.arange(per_owner, dtype=jnp.int32), 0), axis=2)
    take = (cset[..., None] // per_owner == dev).astype(BF16)
    take = jnp.tile(take, (1, 1, 1, 3))
    pick = (target[..., None] == nodes).astype(BF16)
    pick = jnp.tile(pick, (1, 1, 3))
    drop = (target[:, :, None, None, None] == rset[None, None]).astype(BF16)
    drop = jnp.tile(drop, (1, 1, 1, 1, 3)).reshape(LEVELS, n, -1)
    place = (nodes[:, None, None] // per_owner == dev) & (node_level[:, None, None] == every[None, :, None])
    place = jnp.tile(place.astype(BF16), (1, 1, 3)).reshape(ns, -1)

    me = lax.axis_index("dev")
    mine = lambda v: lax.dynamic_slice_in_dim(v, me * per_holder, per_holder, 0)
    mcol, mrow, mlev = mine(tile_column), mine(tile_row), mine(level_of)
    mact = mlev[None] == steps[:, None]
    order = jnp.arange(per_holder, dtype=jnp.int32)
    rank = jnp.sum((mact[:, None, :] & (order[None, :] < order[:, None])).astype(jnp.int32), axis=2)
    chosen = mact[:, None, :] & (rank[:, None, :] == jnp.arange(TCAP, dtype=jnp.int32)[None, :, None])
    c0 = jnp.min(jnp.where(mact, mcol, 1 << 20), axis=1)[:, None]
    r0 = jnp.min(jnp.where(mact, mrow, 1 << 20), axis=1)[:, None]
    pickv = lambda v: jnp.sum(jnp.where(chosen, v, 0), axis=2)
    slot = pickv(jnp.arange(per_holder, dtype=jnp.int32)[None, None, :]) + per_owner
    second = pickv((mcol[None] != c0).astype(jnp.int32)[:, None, :])
    w0 = pickv((mrow[None] == r0).astype(jnp.int32)[:, None, :])
    w1 = pickv((mrow[None] != r0).astype(jnp.int32)[:, None, :])
    table = jnp.stack([slot, second, w0, w1], axis=2).reshape(-1)
    own = lax.dynamic_index_in_dim(own_slot, me, 1, keepdims=False)
    return jnp.concatenate([own, table]), pick, drop, take, place


def per_device(right_sides, diag_inverse, factor_tiles, node_level, tile_column, tile_row):
    n = lax.axis_size("dev")
    per_owner, size = diag_inverse.shape[0], diag_inverse.shape[1]
    per_holder = factor_tiles.shape[0]
    ns = right_sides.shape[1]
    tab, pick, drop, take, place = plan(n, node_level, tile_column, tile_row, per_owner, per_holder)
    mats = per_owner + per_holder
    steps = LEVELS - 1
    phases = 2 * LEVELS + 2 * steps
    vmem = pl.BlockSpec(memory_space=pltpu.VMEM)
    hbm = pl.BlockSpec(memory_space=pl.ANY)
    one = pltpu.VMEM((LEVELS, n, 1, size), F32)
    two = pltpu.VMEM((steps, n, 2, size), F32)
    out = pl.pallas_call(
        functools.partial(kernel, n),
        out_shape=jax.ShapeDtypeStruct((ns, size), F32),
        in_specs=[pl.BlockSpec(memory_space=pltpu.SMEM), vmem, vmem, vmem, vmem, vmem, hbm, hbm],
        out_specs=vmem,
        scratch_shapes=[
            pltpu.VMEM((mats, size, size), F32),
            pltpu.VMEM((mats, size, size), BF16),
            pltpu.VMEM((mats, size, size), BF16),
            pltpu.VMEM((steps * 6 * n, size), BF16),
            pltpu.VMEM((LEVELS * 3 * n, size), BF16),
            one, one, one, one, two, two, two, two,
            pltpu.SemaphoreType.DMA((2,)),
            pltpu.SemaphoreType.DMA((phases,)),
            pltpu.SemaphoreType.DMA((phases,)),
        ],
        compiler_params=pltpu.CompilerParams(
            collective_id=0, has_side_effects=True, vmem_limit_bytes=60 * 1024 * 1024),
    )(tab, pick, drop, take, place, right_sides[0], diag_inverse, factor_tiles)
    return out[None]


def solution(mesh):
    placed = (P("dev", None, None), P("dev", None, None), P("dev", None, None), P(), P(), P())
    return jax.shard_map(
        per_device, mesh=mesh, in_specs=placed, out_specs=P("dev", None, None), check_vma=False
    )
```

time: 302 us -> 126 us (0.42)
  waiting for transfers between devices: 126 us -> 0 us
  Pallas kernels: 0 us -> 112 us
  starting transfers between devices: 65.2 us -> 0 us
  local copies, waits for them, and re-layouts: 59.5 us -> 10.8 us
  matrix products: 23.7 us -> 0 us
  other arithmetic: 15.7 us -> 2.83 us
  between operations: 10.6 us -> 0.16 us
    all_to_all x22 -> x0, waiting for transfers between devices: 126 us -> none  [the longest x4 40.2 us: per_device(): lax.all_to_all(products, 'dev', split_axis=1, concat_axis=1, tiled=True)]
    pallas_call x0 -> x1, Pallas kernels: none -> 112 us  [per_device(): pl.pallas_call(functools.partial(kernel, n), out_shape=jax.ShapeDtypeStru...]
    all_to_all x22 -> x0, starting transfers between devices: 65.2 us -> none  [the longest x5 17.6 us: per_device(): lax.all_to_all(outgoing, 'dev', split_axis=1, concat_axis=1, tiled=True)]
    gather x18 -> x0, local copies, waits for them, and re-layouts: 35.4 us -> none  [the longest x4 24.5 us: per_device(): chosen = jnp.take(factor_tiles, names[0, 0], axis=0)]
    dot_general x9 -> x0, matrix products: 23.7 us -> none  [the longest x4 20.2 us: per_device(): jnp.einsum('rnkb,kbc->rnkc', payload, chosen, precision=full_precision)]
    scatter-add x9 -> x0, other arithmetic: 9.91 us -> none  [scatter_rows(): return field.at[:, placed, :].add(payload, mode='drop')]
    broadcast_in_dim x13 -> x0, local copies, waits for them, and re-layouts: 6.68 us -> none  [the longest x5 3.49 us: per_device(): outgoing = residue[:, :, None, :]]
    another operation x1 -> x10, local copies, waits for them, and re-layouts: 0.01 us -> 4.73 us  [the longest x2 2.18 us: plan(): drop = jnp.tile(drop, (1, 1, 1, 1, 3)).reshape(LEVELS, n, -1)]
  transfers between devices with their start and end apart: 22 -> 0, of which waited for: 22 -> 0; matrix products, arithmetic and copies ran while one was open for 17% -> 0% of each run, Pallas kernels for 0% -> 0%
where the time goes in v1:
time: 126 us; the launch traced here: 125 us
  Pallas kernels  112 us (89%)
  local copies, waits for them, and re-layouts  10.8 us (9%)
  other arithmetic  2.83 us (2%)
    pallas_call x1, Pallas kernels, per_device(): pl.pallas_call(functools.partial(kernel, n), out_shape=jax.ShapeDtypeStru...  112 us

profile of v1, /device:TPU:0, one launch (start us, length us, event | category | flops | bytes accessed | tf_op | source)
XLA Modules:
  0.0 125.4 jit_solution(14621128176969854200)
XLA Ops:
  0.0 0.8 select_reduce_fusion
  0.8 0.1 dynamic_slice.14
  0.9 0.8 dynamic_slice.15
  1.6 0.8 dynamic_slice.16
  2.4 0.1 select_reduce_fusion.12
  2.5 0.1 compare_convert_fusion.1
  2.6 0.1 convert_reduce_fusion
  2.8 0.4 select_reduce_fusion.8
  3.2 0.1 copy.23
  3.3 0.1 reshape.322
  3.4 0.8 eq.177
  4.1 0.1 copy.22
  4.2 0.2 dynamic-slice_reduce_fusion
  4.4 0.6 pad_add_fusion.3.tab
  5.1 0.1 eq.197
  5.1 0.1 copy.24
  5.2 0.8 reshape.326
  6.0 0.1 copy.25
  6.0 0.8 reshape.327
  6.8 0.1 copy.27
  6.9 0.1 select_reduce_fusion.2
  7.0 0.3 compare_convert_fusion
  7.3 0.0 copy-start
  7.3 0.5 tile.36
  7.8 1.7 %tile.37.drop = bf16[5,32,768]{2,1,0:T(8,128)(2,1)} reshape(bf16[5,32,4,1,2,3,32]{6,5,4,2,1,0,3:T(4,128)(2,1)S(1)} %tile.36) | data formatting | bytes 491520 | tf_op jit(solution)/shard_map/tile | solution.py:181
  9.5 0.1 fusion
  9.6 0.1 tile.38
  9.7 0.8 tile.39.take
  10.5 0.1 fusion.1
  10.6 0.8 tile.17.pick
  11.4 0.0 copy-done
  11.5 0.7 copy.29.place
  12.2 111.6 %shard_map.64 = f32[64,512]{1,0:T(8,128)} custom-call(s32[69]{0:T(128)} %pad_add_fusion.3.tab, bf16[5,32,192]{2,1,0:T(8,128)(2,1)} %tile.17.pick, bf16[5,32,768]{2,1,0:T(8,128)(2,1)} %tile.37.drop, bf16[4,2,32,96]{3,2,1,0:T(8,128)(2,1)} %tile.39.take, bf16[64,480]{1,0:T(8,128)(2,1)} %copy.29.place, f32[64,512]{1,0:T(8,128)} %bitcast.16, ...), custom_call_target="tpu_custom_call" | custom-call | tf_op jit(solution)/shard_map/pallas_call | solution.py:217
  123.8 1.6 %copy.31 = f32[1,64,512]{2,1,0:T(8,128)} copy(f32[1,64,512]{2,1,0:T(8,128)} %bitcast.14) | data formatting | bytes 262144
  (16 shorter events, 0.2 us)
Async XLA Ops:
  7.3 4.2 %copy-start = (s32[64]{0:T(128)S(1)}, s32[64]{0:T(128)}, u32[]{:S(2)}) copy-start(s32[64]{0:T(128)} %param.9) | copy-start | bytes 772
